TPU v7x, 128 devices: a whole 4x4x4 slice. The times are simulated.
128 devices in a mesh: tile: 16 (over x, y), scan: 8 (over z, core).
Axes of the slice: x: 4, y: 4, z: 4, core: 2. Of those that a mesh axis runs over, the one named last changes fastest.
Arguments:
- object_field: float32 [2, 16384, 1024], P(None, 'tile'), may hold values from -6 to 6
- probe: float32 [2, 512, 512], replicated, may hold values from -6 to 6
- amplitudes: float32 [384, 512, 512], P(('tile', 'scan')), may hold values from 0 to 3
- corners: int32 [384, 2], P(('tile', 'scan')), may hold values from 0 to 16383, as said below
Outputs:
- object_gradient: float32 [2, 16384, 1024], P(None, 'tile')
- probe_gradient: float32 [2, 512, 512], replicated
Inputs may be any that keep to these rules, and one draw needn't show every extreme that they name: `corners`: pattern n belongs to tile n // 24, and its corner row lies in that tile's rows: from (n // 24) * 1024 to that plus 1024 - 1; its corner column lies in 0 to 512.
All inputs are finite; a program needn't handle non-finite values.
Results may differ from a plain program's by a relative error of at most 0.0003.
Values sent between devices are 32-bit elements; how exact they have to be, the bound alone decides.
No kernel may reach another device: no remote copies, remote signals or barrier semaphores. Data moves between devices by JAX's collectives and lax.ppermute only.
A program may use at most 192 MiB of HBM per device.

v0:
```python
from functools import partial
import math

import jax
import jax.numpy as jnp
from jax import lax
from jax.sharding import PartitionSpec as P


def passed_along(block, axis, distance):
    devices = range(lax.axis_size(axis))
    route = [(i - distance, i) for i in devices if i - distance in devices]
    return lax.ppermute(block, axis, route)


def dft_tables(patch_size):
    indices = jnp.arange(patch_size, dtype=jnp.int32)
    phase = indices[:, None] * indices[None, :] % patch_size
    phase_angle = phase.astype(jnp.float32) * (2.0 * math.pi / patch_size)
    norm_scale = 1.0 / math.sqrt(patch_size)
    return (jnp.cos(phase_angle) * norm_scale, -jnp.sin(phase_angle) * norm_scale)


def complex_product(left_real, left_imag, right_real, right_imag):
    product = partial(jnp.matmul, precision=lax.Precision.HIGHEST)
    return (
        product(left_real, right_real) - product(left_imag, right_imag),
        product(left_real, right_imag) + product(left_imag, right_real),
    )


def transform(field_real, field_imag, table_real, table_imag):
    inner_real, inner_imag = complex_product(table_real, table_imag, field_real, field_imag)
    return complex_product(inner_real, inner_imag, table_real, table_imag)


def pattern_terms(patch, probe, amplitude, table_real, table_imag):
    probe_real, probe_imag = (probe[0], probe[1])
    patch_real, patch_imag = (patch[0], patch[1])
    wave_real = probe_real * patch_real - probe_imag * patch_imag
    wave_imag = probe_real * patch_imag + probe_imag * patch_real
    far_real, far_imag = transform(wave_real, wave_imag, table_real, table_imag)
    modulus = jnp.sqrt(far_real * far_real + far_imag * far_imag + 1.0)
    factor = 1.0 - amplitude / modulus
    error_real, error_imag = transform(
        far_real * factor, far_imag * factor, table_real, -table_imag
    )
    object_term = jnp.stack(
        [
            probe_real * error_real + probe_imag * error_imag,
            probe_real * error_imag - probe_imag * error_real,
        ]
    )
    probe_term = jnp.stack(
        [
            patch_real * error_real + patch_imag * error_imag,
            patch_real * error_imag - patch_imag * error_real,
        ]
    )
    return (object_term, probe_term)


def fold_lower(window, strip_rows, patch_size, received):
    owned = window[:, :strip_rows, :]
    return jnp.concatenate([owned[:, :patch_size, :] + received, owned[:, patch_size:, :]], axis=1)


def on_device(object_field, probe, amplitudes, corners):
    strip_rows = object_field.shape[1]
    full_cols = object_field.shape[2]
    patch_size = probe.shape[1]
    pattern_count = amplitudes.shape[0]
    table_real, table_imag = dft_tables(patch_size)
    row_starts = corners[:, 0] - lax.axis_index("tile") * strip_rows
    col_starts = corners[:, 1]
    zero_index = jnp.zeros((), jnp.int32)
    following = passed_along(object_field, "tile", -1)
    extended = jnp.concatenate([object_field, following], axis=1)

    def cut_patch(pattern_index):
        anchor = (zero_index, row_starts[pattern_index], col_starts[pattern_index])
        return lax.dynamic_slice(extended, anchor, (2, patch_size, patch_size))

    def accumulate(totals, pattern_index):
        window, probe_sum = totals
        patch = cut_patch(pattern_index)
        object_term, probe_term = pattern_terms(
            patch, probe, amplitudes[pattern_index], table_real, table_imag
        )
        anchor = (zero_index, row_starts[pattern_index], col_starts[pattern_index])
        previous = lax.dynamic_slice(window, anchor, (2, patch_size, patch_size))
        window = lax.dynamic_update_slice(window, previous + object_term, anchor)
        return ((window, probe_sum + probe_term), None)

    empty_window = jnp.zeros((2, strip_rows + patch_size, full_cols), jnp.float32)
    start_totals = (empty_window, jnp.zeros(probe.shape, jnp.float32))
    (window, probe_sum), unused = lax.scan(
        accumulate, start_totals, jnp.arange(pattern_count, dtype=jnp.int32)
    )
    lower = window[:, strip_rows:, :]
    received = passed_along(lower, "tile", 1)
    owned = fold_lower(window, strip_rows, patch_size, received)
    object_gradient = lax.psum(owned, "scan")
    probe_gradient = lax.psum(probe_sum, ("tile", "scan"))
    return (object_gradient, probe_gradient)


def solution(mesh):
    placed = (
        P(None, "tile", None),
        P(),
        P(("tile", "scan"), None, None),
        P(("tile", "scan"), None),
    )
    return jax.shard_map(
        on_device,
        mesh=mesh,
        in_specs=placed,
        out_specs=(P(None, "tile", None), P()),
        check_vma=False,
    )
```

profile of v0, /device:TPU:1, one launch (start us, length us, event | category | flops | bytes accessed | tf_op | source)
XLA Modules:
  0.0 1035.1 jit_solution(10410323029884733683)
XLA Ops:
  9.3 182.0 %collective-permute-done = f32[2,1024,1024]{2,1,0:T(8,128)} collective-permute-done((f32[2,1024,1024]{2,1,0:T(8,128)}, f32[2,1024,1024]{2,1,0:T(8,128)}, u32[]{:S(2)}, u32[]{:S(2)}) %collective-permute-start) | collective-permute-done | bytes 8388640 | tf_op jit(solution)/shard_map/ppermute | solution.py:13
  191.3 11.7 %pad_maximum_fusion = f32[2,2048,1024]{2,1,0:T(8,128)} fusion(f32[2,1024,1024]{2,1,0:T(8,128)} %collective-permute-done, f32[2,1024,1024]{2,1,0:T(8,128)} %param.6), kind=kLoop, calls=%fused_computation.138 | loop fusion | flops 4194304 | bytes 33554432 | tf_op jit(solution)/shard_map/concatenate | solution.py:78
  209.2 479.6 %while.15 = (s32[]{:T(128)}, f32[2,1536,1024]{2,1,0:T(8,128)}, f32[2,512,512]{2,1,0:T(8,128)}, s32[3]{0:T(128)S(1)}, s32[3]{0:T(128)S(1)}, /*index=5*/s32[3]{0:T...) while((s32[]{:T(128)}, f32[2,1536,1024]{2,1,0:T(8,128)}, ...), condition=%wide.region_1.2_spmd.clone.clone, body=%wide.region_0.1_spmd.clone.clone.sunk | while | flops 25847398400 | bytes 93323696 | solution.py:97
  243.9 8.2 convolution_add_fusion.6
  267.4 7.8 convolution_subtract_fusion.9
  275.2 9.4 fusion.184
  292.3 7.9 convolution_subtract_fusion.10
  315.4 8.0 fusion.188
  331.0 7.7 convolution_subtract_fusion.11
  338.7 10.5 %add_bitcast_fusion.2 = (f32[1,512,512]{2,1,0:T(8,128)S(1)}, f32[1,512,512]{2,1,0:T(8,128)S(1)}, f32[1,512,512]{2,1,0:T(8,128)S(1)}, f32[1,512,512]{2,1,0:T(8,128)S(1)}) fusion(f32[512,512]{1,0:T(8,128)S(1)} %convolution_subtract_fusion.11, f32[2,2048,1024]{2,1,0:T(8,128)} %get-tuple-element.378, s32[]{:T(128)S(6)} %select_n.155, ...), kind=kOutput, calls=%fused_computation.42.clone.1 | convolution fusion | flops 1617952768 | bytes 11534348 | tf_op jit(solution)/shard_map/while/body/eval_jaxpr/dot_general | solution.py:28
  353.6 14.1 %dynamic_update_slice.7 = f32[2,1536,1024]{2,1,0:T(8,128)} dynamic-update-slice(f32[2,1536,1024]{2,1,0:T(8,128)} %get-tuple-element.356, f32[2,512,512]{2,1,0:T(8,128)S(1)} %get-tuple-element.337, s32[]{:T(128)} %constant.47.clone.1..sunk, s32[]{:T(128)S(6)} %select_n.157, s32[]{:T(128)S(6)} %select_n.156) | dynamic-update-slice | bytes 4194308 | tf_op jit(solution)/shard_map/while/body/eval_jaxpr/dynamic_update_slice | solution.py:92
  402.7 8.0 convolution_add_fusion.6
  426.0 7.8 convolution_subtract_fusion.9
  433.8 9.4 fusion.184
  450.9 7.9 convolution_subtract_fusion.10
  474.0 8.0 fusion.188
  489.6 7.7 convolution_subtract_fusion.11
  497.3 10.5 %add_bitcast_fusion.2 = (f32[1,512,512]{2,1,0:T(8,128)S(1)}, f32[1,512,512]{2,1,0:T(8,128)S(1)}, f32[1,512,512]{2,1,0:T(8,128)S(1)}, f32[1,512,512]{2,1,0:T(8,128)S(1)}) fusion(f32[512,512]{1,0:T(8,128)S(1)} %convolution_subtract_fusion.11, f32[2,2048,1024]{2,1,0:T(8,128)} %get-tuple-element.378, s32[]{:T(128)S(6)} %select_n.155, ...), kind=kOutput, calls=%fused_computation.42.clone.1 | convolution fusion | flops 1617952768 | bytes 11534348 | tf_op jit(solution)/shard_map/while/body/eval_jaxpr/dot_general | solution.py:28
  512.2 14.2 %dynamic_update_slice.7 = f32[2,1536,1024]{2,1,0:T(8,128)} dynamic-update-slice(f32[2,1536,1024]{2,1,0:T(8,128)} %get-tuple-element.356, f32[2,512,512]{2,1,0:T(8,128)S(1)} %get-tuple-element.337, s32[]{:T(128)} %constant.47.clone.1..sunk, s32[]{:T(128)S(6)} %select_n.157, s32[]{:T(128)S(6)} %select_n.156) | dynamic-update-slice | bytes 4194308 | tf_op jit(solution)/shard_map/while/body/eval_jaxpr/dynamic_update_slice | solution.py:92
  561.5 8.0 convolution_add_fusion.6
  569.5 7.6 fusion.183
  584.7 7.8 convolution_subtract_fusion.9
  592.6 9.4 fusion.184
  609.6 7.9 convolution_subtract_fusion.10
  632.7 8.0 fusion.188
  648.4 7.7 convolution_subtract_fusion.11
  656.1 10.5 %add_bitcast_fusion.2 = (f32[1,512,512]{2,1,0:T(8,128)S(1)}, f32[1,512,512]{2,1,0:T(8,128)S(1)}, f32[1,512,512]{2,1,0:T(8,128)S(1)}, f32[1,512,512]{2,1,0:T(8,128)S(1)}) fusion(f32[512,512]{1,0:T(8,128)S(1)} %convolution_subtract_fusion.11, f32[2,2048,1024]{2,1,0:T(8,128)} %get-tuple-element.378, s32[]{:T(128)S(6)} %select_n.155, ...), kind=kOutput, calls=%fused_computation.42.clone.1 | convolution fusion | flops 1617952768 | bytes 11534348 | tf_op jit(solution)/shard_map/while/body/eval_jaxpr/dot_general | solution.py:28
  671.0 14.2 %dynamic_update_slice.7 = f32[2,1536,1024]{2,1,0:T(8,128)} dynamic-update-slice(f32[2,1536,1024]{2,1,0:T(8,128)} %get-tuple-element.356, f32[2,512,512]{2,1,0:T(8,128)S(1)} %get-tuple-element.337, s32[]{:T(128)} %constant.47.clone.1..sunk, s32[]{:T(128)S(6)} %select_n.157, s32[]{:T(128)S(6)} %select_n.156) | dynamic-update-slice | bytes 4194308 | tf_op jit(solution)/shard_map/while/body/eval_jaxpr/dynamic_update_slice | solution.py:92
  699.1 90.0 %collective-permute-done.1 = f32[2,512,1024]{2,1,0:T(8,128)} collective-permute-done((f32[2,512,1024]{2,1,0:T(8,128)}, f32[2,512,1024]{2,1,0:T(8,128)}, u32[]{:S(2)}, u32[]{:S(2)}) %collective-permute-start.1) | collective-permute-done | bytes 4194336 | tf_op jit(solution)/shard_map/ppermute | solution.py:13
  799.5 113.7 %all-reduce.5.cloned.1.call-done = f32[2,512,512]{2,1,0:T(8,128)} async-done(((f32[2,512,512]{2,1,0:T(8,128)}), f32[2,512,512]{2,1,0:T(8,128)}) %all-reduce.5.cloned.1.call-update) | async-done | bytes 2097168 | tf_op jit(solution)/shard_map/psum | solution.py:104
  913.2 105.0 %all-reduce.3.cloned.1.call-done = f32[2,1024,1024]{2,1,0:T(8,128)} async-done(((f32[2,1024,1024]{2,1,0:T(8,128)}), f32[2,1024,1024]{2,1,0:T(8,128)}) %all-reduce.3.cloned.1.call-update) | async-done | bytes 8388624 | tf_op jit(solution)/shard_map/psum | solution.py:103
  1018.2 8.4 copy.18
  (69 shorter events, 255.8 us)
Async XLA Ops:
  7.2 906.0 %all-reduce.5.cloned.1.call-start = ((), (), s32[]{:S(2)}) async-start(), calls=%async_computation.1 | async-start | bytes 4194304 | tf_op jit(solution)/shard_map/psum | solution.py:104
  7.2 184.1 %collective-permute-start = (f32[2,1024,1024]{2,1,0:T(8,128)}, f32[2,1024,1024]{2,1,0:T(8,128)}, u32[]{:S(2)}, u32[]{:S(2)}) collective-permute-start(f32[2,1024,1024]{2,1,0:T(8,128)} %param.6), channel_id=1, source_target_pairs={{8,0},{16,8},{24,16},{32,24},{40,32},{48,40},{56,48},{64,56},{72,6... | collective-permute-start | bytes 25165832 | tf_op jit(solution)/shard_map/ppermute | solution.py:13
  338.7 10.5 %copy-start = (f32[2,512,512]{2,1,0:T(8,128)S(1)}, f32[2,512,512]{2,1,0:T(8,128)}, u32[]{:S(2)}) copy-start(f32[2,512,512]{2,1,0:T(8,128)} %get-tuple-element.357) | copy-start | bytes 6291460 | tf_op jit(solution)/shard_map/while
  352.3 1.3 copy-start.1
  497.3 10.5 %copy-start = (f32[2,512,512]{2,1,0:T(8,128)S(1)}, f32[2,512,512]{2,1,0:T(8,128)}, u32[]{:S(2)}) copy-start(f32[2,512,512]{2,1,0:T(8,128)} %get-tuple-element.357) | copy-start | bytes 6291460 | tf_op jit(solution)/shard_map/while
  510.9 1.3 copy-start.1
  656.0 10.5 %copy-start = (f32[2,512,512]{2,1,0:T(8,128)S(1)}, f32[2,512,512]{2,1,0:T(8,128)}, u32[]{:S(2)}) copy-start(f32[2,512,512]{2,1,0:T(8,128)} %get-tuple-element.357) | copy-start | bytes 6291460 | tf_op jit(solution)/shard_map/while
  669.7 1.3 copy-start.1
  693.6 95.6 %collective-permute-start.1 = (f32[2,512,1024]{2,1,0:T(8,128)}, f32[2,512,1024]{2,1,0:T(8,128)}, u32[]{:S(2)}, u32[]{:S(2)}) collective-permute-start(f32[2,512,1024]{2,1,0:T(8,128)} %slice.37), channel_id=1, source_target_pairs={{0,8},{8,16},{16,24},{24,32},{32,40},{40,48},{48,56},{56,64},{64,7... | collective-permute-start | bytes 12582920 | tf_op jit(solution)/shard_map/ppermute | solution.py:13
  699.1 319.1 %all-reduce.3.cloned.1.call-start = ((), (), s32[]{:S(2)}) async-start(), calls=%async_computation | async-start | bytes 16777216 | tf_op jit(solution)/shard_map/psum | solution.py:103
  913.2 113.5 %copy-start.2 = (f32[2,512,512]{2,1,0:T(8,128)S(1)}, f32[2,512,512]{2,1,0:T(8,128)}, u32[]{:S(2)}) copy-start(f32[2,512,512]{2,1,0:T(8,128)} %all-reduce.5.cloned.1.call-done) | copy-start | bytes 6291460
Sparse Core Ops, SparseCore 0:
  699.2 213.9 all-reduce.4
  916.1 102.0 all-reduce.2
where the time goes:
time: 1040 us
  waiting for transfers between devices  491 us (47%)
  matrix products  383 us (37%)
  local copies, waits for them, and re-layouts  73.1 us (7%)
  other arithmetic  41 us (4%)
  loops' own time  25.5 us (2%)
  between operations  14.3 us (1%)
    ppermute x2, waiting for transfers between devices, passed_along(): return lax.ppermute(block, axis, route)  272 us
    psum x1, waiting for transfers between devices, on_device(): probe_gradient = lax.psum(probe_sum, ('tile', 'scan'))  114 us
    dot_general x12, matrix products, complex_product(): product(left_imag, right_real)  107 us
    psum x1, waiting for transfers between devices, on_device(): object_gradient = lax.psum(owned, 'scan')  105 us
    dot_general x12, matrix products, complex_product(): product(left_imag, right_imag)  93 us
    dot_general x12, matrix products, complex_product(): product(left_real, right_imag) + product(left_imag, right_real)  92.5 us
    dot_general x12, matrix products, complex_product(): product(left_real, right_real) - product(left_imag, right_imag)  91 us
    dynamic_update_slice x3, local copies, waits for them, and re-layouts, accumulate(): window = lax.dynamic_update_slice(window, previous + object_term, anchor)  42.6 us
  transfers between devices with their start and end apart: 4, of which 4 were waited for; matrix products, arithmetic and copies ran while one was open for 1% of the time, Pallas kernels for 0%

commit v1 on v0

v1 whole, which is shorter than its diff:
```python
import functools
import math

import jax
import jax.numpy as jnp
import ml_dtypes
import numpy as np
from jax import lax
from jax.experimental import pallas as pl
from jax.experimental.pallas import tpu as pltpu
from jax.sharding import Mesh, PartitionSpec as P

SIDE = 512
QUART = 128
COLS = 1024
STRIP = 1024
SPAN = STRIP + SIDE
SLICE = 64
CHUNK = 64
PAT = 3
ROUTE = (
    (2, 0, 0, (0, 0)),
    (1, 1, 0, (0, 1)),
    (3, 0, 0, (1, 0)),
    (2, 1, 0, (1, 1)),
    (1, 0, 1, (0,)),
    (3, 1, 1, (1,)),
    (0, 0, 1, (2,)),
    (0, 1, 1, (3,)),
)
BF = jnp.bfloat16
F32 = jnp.float32


def quarter_tables():
    k0 = np.arange(4)[:, None, None]
    k1 = np.arange(QUART)[None, :, None]
    i0 = np.arange(QUART)[None, None, :]
    phase = ((4 * k1 + k0) * i0) % SIDE
    angle = phase.astype(np.float64) * (2.0 * math.pi / SIDE)
    real = np.cos(angle) / math.sqrt(SIDE)
    imag = -np.sin(angle) / math.sqrt(SIDE)
    form = np.concatenate(
        [np.concatenate([real, -imag], axis=2), np.concatenate([imag, real], axis=2)], axis=1
    ).astype(np.float32)

    def parts(table):
        high = table.astype(ml_dtypes.bfloat16)
        low = (table - high.astype(np.float32)).astype(ml_dtypes.bfloat16)
        return np.stack([high, low])

    return parts(form), parts(np.ascontiguousarray(np.swapaxes(form, 1, 2)))


def order_matrix():
    index = np.arange(SIDE)
    order = 4 * (index % QUART) + index // QUART
    return (order[:, None] == index[None, :]).astype(np.float32)


def split(value):
    high = value.astype(BF)
    return high, (value - high.astype(F32)).astype(BF)


def dot3(left_high, left_low, right_high, right_low):
    dot = functools.partial(jnp.dot, preferred_element_type=F32)
    return dot(left_high, right_high) + (dot(left_high, right_low) + dot(left_low, right_high))


def radix4(parts, sign):
    (r0, i0), (r1, i1), (r2, i2), (r3, i3) = parts
    ar, ai, br, bi = r0 + r2, i0 + i2, r0 - r2, i0 - i2
    cr, ci, dr, di = r1 + r3, i1 + i3, r1 - r3, i1 - i3
    plus = (br - di, bi + dr)
    minus = (br + di, bi - dr)
    first, third = (plus, minus) if sign > 0 else (minus, plus)
    return [(ar + cr, ai + ci), first, (ar - cr, ai - ci), third]


def patterns_kernel(where, strip, *refs):
    halo = refs[:10]
    probe, amps, form, flip = refs[10:14]
    sends = refs[14:22]
    probe_sum = refs[22]
    ext, win, patch, high, low, real, sems = refs[23:]
    z = where[6]
    core = where[7]

    copies = []

    def start(src, dst):
        copy = pltpu.make_async_copy(src, dst, sems.at[len(copies)])
        copy.start()
        copies.append(copy)

    start(strip, ext.at[:, pl.ds(0, STRIP), :])
    for half, owner in ((0, core), (1, 1 - core)):
        pieces = halo[5 * half : 5 * half + 5]

        def place(q):
            row = STRIP + lax.rem(z + q, 4) * (2 * SLICE) + owner * SLICE
            return pl.ds(pl.multiple_of(row, SLICE), SLICE)

        start(pieces[0], ext.at[:, place(0), :])
        start(pieces[1], ext.at[:, place(3), :])
        start(pieces[2], ext.at[:, place(1), :])
        start(pieces[3], ext.at[0, place(2), :])
        start(pieces[4], ext.at[1, place(2), :])

    def clear(step, carry):
        win[:, pl.ds(pl.multiple_of(step * CHUNK, CHUNK), CHUNK), :] = jnp.zeros((2, CHUNK, COLS), F32)
        return carry

    lax.fori_loop(0, SPAN // CHUNK, clear, 0)
    probe_sum[...] = jnp.zeros_like(probe_sum)
    for copy in copies:
        copy.wait()

    def one_pattern(p, carry):
        row = where[2 * p]
        col = where[2 * p + 1]
        row8 = pl.multiple_of((row // 8) * 8, 8)
        col128 = pl.multiple_of(jnp.minimum((col // QUART) * QUART, COLS - SIDE - QUART), QUART)
        row_off = row - row8
        col_off = col - col128

        def cut(step, carry):
            base = pl.multiple_of(step * CHUNK, CHUNK)
            rows = pl.ds(base, CHUNK)
            cuts = []
            for plane in range(2):
                block = ext[plane, pl.ds(pl.multiple_of(row8 + base, 8), CHUNK + 8), pl.ds(col128, SIDE + QUART)]
                block = pltpu.roll(block, lax.rem(CHUNK + 8 - row_off, CHUNK + 8), 0)[:CHUNK]
                block = pltpu.roll(block, lax.rem(SIDE + QUART - col_off, SIDE + QUART), 1)[:, :SIDE]
                patch[plane, rows, :] = block
                cuts.append(block)
            pr, pi = probe[0, rows, :], probe[1, rows, :]
            wr = pr * cuts[0] - pi * cuts[1]
            wi = pr * cuts[1] + pi * cuts[0]
            terms = radix4([(wr[:, n * QUART : (n + 1) * QUART], wi[:, n * QUART : (n + 1) * QUART]) for n in range(4)], -1)
            for n, (tr, ti) in enumerate(terms):
                hr, lr = split(tr)
                hi, li = split(ti)
                high[n, rows, :QUART] = hr
                high[n, rows, QUART:] = hi
                low[n, rows, :QUART] = lr
                low[n, rows, QUART:] = li
            return carry

        lax.fori_loop(0, SIDE // CHUNK, cut, 0)

        for n in range(4):
            real[pl.ds(n * SIDE, SIDE), :] = dot3(high[n], low[n], flip[0, n], flip[1, n])

        for n in range(4):
            lanes = pl.ds((n % 2) * QUART, QUART)

            def rows_in(step, carry):
                base = pl.multiple_of(step * 32, 32)
                parts = []
                for m in range(4):
                    block = real[pl.ds(pl.multiple_of(n * SIDE + m * QUART + base, 32), 32), :]
                    parts.append((block[:, :QUART], block[:, QUART:]))
                for m, (tr, ti) in enumerate(radix4(parts, -1)):
                    hr, lr = split(tr)
                    hi, li = split(ti)
                    at_re = pl.ds(pl.multiple_of((n // 2) * 256 + base, 32), 32)
                    at_im = pl.ds(pl.multiple_of((n // 2) * 256 + QUART + base, 32), 32)
                    high[m, at_re, lanes] = hr
                    high[m, at_im, lanes] = hi
                    low[m, at_re, lanes] = lr
                    low[m, at_im, lanes] = li
                return carry

            lax.fori_loop(0, QUART // 32, rows_in, 0)

        for m in range(4):
            for half in range(2):
                at = pl.ds(half * 256, 256)
                far = dot3(form[0, m], form[1, m], high[m, at, :], low[m, at, :])
                fr, fi = far[:QUART], far[QUART:]
                amp = amps[p, pl.ds(m * QUART, QUART), pl.ds(half * 256, 256)]
                factor = 1.0 - amp * lax.rsqrt(fr * fr + fi * fi + 1.0)
                hr, lr = split(fr * factor)
                hi, li = split(fi * factor)
                right_high = jnp.concatenate([hr, hi], axis=0)
                right_low = jnp.concatenate([lr, li], axis=0)
                real[pl.ds(m * SIDE + half * 256, 256), :] = dot3(flip[0, m], flip[1, m], right_high, right_low)

        for n in range(4):
            half, lane = n // 2, (n % 2) * QUART

            def rows_out(step, carry):
                base = pl.multiple_of(step * 32, 32)
                parts = []
                for m in range(4):
                    at_re = pl.ds(pl.multiple_of(m * SIDE + half * 256 + base, 32), 32)
                    at_im = pl.ds(pl.multiple_of(m * SIDE + half * 256 + QUART + base, 32), 32)
                    parts.append((real[at_re, pl.ds(lane, QUART)], real[at_im, pl.ds(lane, QUART)]))
                for m, (tr, ti) in enumerate(radix4(parts, 1)):
                    hr, lr = split(tr)
                    hi, li = split(ti)
                    at = pl.ds(pl.multiple_of(m * QUART + base, 32), 32)
                    high[n, at, :QUART] = hr
                    high[n, at, QUART:] = hi
                    low[n, at, :QUART] = lr
                    low[n, at, QUART:] = li
                return carry

            lax.fori_loop(0, QUART // 32, rows_out, 0)

        for n in range(4):
            real[pl.ds(n * SIDE, SIDE), :] = dot3(high[n], low[n], form[0, n], form[1, n])

        def finish(step, carry):
            base = pl.multiple_of(step * CHUNK, CHUNK)
            rows = pl.ds(base, CHUNK)
            parts = []
            for n in range(4):
                block = real[pl.ds(pl.multiple_of(n * SIDE + base, CHUNK), CHUNK), :]
                parts.append((block[:, :QUART], block[:, QUART:]))
            blocks = radix4(parts, 1)
            er = jnp.concatenate([b[0] for b in blocks], axis=1)
            ei = jnp.concatenate([b[1] for b in blocks], axis=1)
            qr, qi = patch[0, rows, :], patch[1, rows, :]
            probe_sum[0, rows, :] += qr * er + qi * ei
            probe_sum[1, rows, :] += qr * ei - qi * er
            pr, pi = probe[0, rows, :], probe[1, rows, :]
            terms = (pr * er + pi * ei, pr * ei - pi * er)
            for plane in range(2):
                wide = jnp.concatenate([terms[plane], jnp.zeros((CHUNK, QUART), F32)], axis=1)
                wide = pltpu.roll(wide, col_off, 1)
                tall = jnp.concatenate([wide, jnp.zeros((8, SIDE + QUART), F32)], axis=0)
                tall = pltpu.roll(tall, row_off, 0)
                at = (plane, pl.ds(pl.multiple_of(row8 + base, 8), CHUNK + 8), pl.ds(col128, SIDE + QUART))
                win[at] = win[at] + tall
            return carry

        lax.fori_loop(0, SIDE // CHUNK, finish, 0)
        return carry

    lax.fori_loop(0, PAT, one_pattern, 0)

    first = len(copies)
    for zone in (2, 0, 1):
        for j, plane, group, at in ROUTE:
            top = zone * SIDE + lax.rem(z + j, 4) * (2 * SLICE)
            for which, owner in ((0, 1 - core), (1, core)):
                rows = pl.ds(pl.multiple_of(top + owner * SLICE, SLICE), SLICE)
                dst = sends[6 + which].at[at + (zone,)] if group else sends[2 * zone + which].at[at]
                start(win.at[plane, rows, :], dst)
    for copy in copies[first:]:
        copy.wait()


def run_patterns(where, strip, halo, probe, amps):
    form, flip = quarter_tables()
    hbm = pl.BlockSpec(memory_space=pl.ANY)
    vmem = pl.BlockSpec(memory_space=pltpu.VMEM)
    smem = pl.BlockSpec(memory_space=pltpu.SMEM)
    leads = [(2, 2)] * 6 + [(4, 3)] * 2
    part = [jax.ShapeDtypeStruct(lead + (SLICE, COLS), F32) for lead in leads]
    return pl.pallas_call(
        patterns_kernel,
        out_shape=part + [jax.ShapeDtypeStruct((2, SIDE, SIDE), F32)],
        in_specs=[smem, hbm] + [hbm] * 10 + [vmem] * 4,
        out_specs=[hbm] * 8 + [vmem],
        scratch_shapes=[
            pltpu.VMEM((2, SPAN, COLS), F32),
            pltpu.VMEM((2, SPAN, COLS), F32),
            pltpu.VMEM((2, SIDE, SIDE), F32),
            pltpu.VMEM((4, SIDE, 256), BF),
            pltpu.VMEM((4, SIDE, 256), BF),
            pltpu.VMEM((4 * SIDE, 256), F32),
            pltpu.SemaphoreType.DMA((64,)),
        ],
        compiler_params=pltpu.CompilerParams(vmem_limit_bytes=56 * 1024 * 1024),
        cost_estimate=pl.CostEstimate(flops=2 * 4_831_838_208, bytes_accessed=40_000_000, transcendentals=786_432),
    )(where, strip, *halo, probe, amps, jnp.asarray(form), jnp.asarray(flip))


def ring(axis, step):
    size = lax.axis_size(axis)
    return [(i, (i + step) % size) for i in range(size)]


def z_up(block):
    return lax.ppermute(block, "z", ring("z", 1))


def z_down(block):
    return lax.ppermute(block, "z", ring("z", -1))


def swap(block):
    return lax.ppermute(block, "core", [(0, 1), (1, 0)])


def along_tiles(block, step):
    tiles = lax.axis_size("x") * lax.axis_size("y")
    return lax.ppermute(block, ("x", "y"), [(i, i + step) for i in range(tiles) if 0 <= i + step < tiles])


def spread(own):
    below = z_up(own)
    above = z_down(own)
    return [own, below, above, z_up(below[0]), z_down(above[1])]


def first_half(theirs, mine):
    both = mine + swap(theirs)
    return z_up(both[0]), z_down(both[1])


def second_half(both, from_below, from_above):
    last_below = z_up(both[0] + from_below[0])
    last_above = z_down(both[1] + from_above[1])
    return both[2] + from_above[0] + last_below, both[3] + from_below[1] + last_above


def others(block, axis):
    return [lax.ppermute(block, axis, ring(axis, -step)) for step in (1, 2, 3)]


def in_order(block, axis, rest=None):
    here = lax.axis_index(axis)
    four = jnp.stack([block] + (rest or others(block, axis)), axis=1)
    four = lax.dynamic_slice_in_dim(jnp.concatenate([four, four], axis=1), lax.rem(4 - here, 4), 4, 1)
    return four.reshape(2, -1, block.shape[2])


def share_of_sum(part, axis):
    here = lax.axis_index(axis)
    cut = part.reshape(2, 4, -1, part.shape[2])
    mine = lax.dynamic_index_in_dim(cut, here, 1, keepdims=False)
    return mine, [
        lax.ppermute(
            lax.dynamic_index_in_dim(cut, lax.rem(here + step, 4), 1, keepdims=False), axis, ring(axis, step)
        )
        for step in (1, 2, 3)
    ]


def on_device(object_field, probe, amplitudes, corners):
    z = lax.axis_index("z")
    core = lax.axis_index("core")
    tile = lax.axis_index("x") * lax.axis_size("y") + lax.axis_index("y")
    local = corners - jnp.array([1, 0], jnp.int32) * (tile * STRIP)
    where = jnp.concatenate([local.reshape(-1), jnp.stack([z, core]).astype(jnp.int32)])

    share = lax.dynamic_slice(
        object_field, (0, z * (2 * SLICE) + core * SLICE, 0), (2, SLICE, COLS)
    )
    order = jnp.asarray(order_matrix())
    product = functools.partial(jnp.einsum, precision=lax.Precision.HIGH)
    amps = product("nkl,ml->nkm", product("mk,nkl->nml", order, amplitudes), order)
    shifted, amps = lax.optimization_barrier((along_tiles(share, -1), amps))
    pieces = spread(shifted)
    halo = pieces + [swap(piece) for piece in pieces]

    *sends, theirs2, mine2, probe_sum = run_patterns(where, object_field, halo, probe, amps)

    tie = lax.optimization_barrier
    halves = probe_sum.reshape(2, 2, SIDE // 2, SIDE)
    part = lax.dynamic_index_in_dim(halves, core, 1, keepdims=False)
    part = part + swap(lax.dynamic_index_in_dim(halves, 1 - core, 1, keepdims=False))

    first_low = first_half(sends[4], sends[5])
    first_top = first_half(sends[0], sends[1])
    first_mid = first_half(sends[2], sends[3])
    both2 = mine2 + swap(theirs2)
    first_low, part = tie((first_low, part))
    low = second_half(both2[:, 2], *first_low)
    part, pieces = share_of_sum(part, "y")
    first_top, part, pieces = tie((first_top, part, pieces))
    part, pieces = share_of_sum(sum(pieces, part), "x")
    first_mid, part, pieces, low = tie((first_mid, part, pieces, low))
    carried = along_tiles(jnp.stack(low), 1)
    below, above = (jnp.stack(pair, axis=1) for pair in zip(first_top, first_mid))
    part = sum(pieces, part)
    below, above, part, pieces = tie((below, above, part, others(part, "z")))
    part = in_order(sum(pieces, part), "x")
    re, im = second_half(both2[:, :2], below, above)
    re, im, part, carried = tie((re, im, part, carried))

    re = re.at[0].add(carried[0])
    im = im.at[0].add(carried[1])
    re, im = tie((re, im))
    below_re, above_im = z_up(re), z_down(im)
    below_im, above_re = z_up(im), z_down(re)
    opposite_re, opposite_im = z_up(below_re), z_down(above_im)
    found = (
        (re, 0, 0), (im, 1, 0),
        (below_re, 0, 3), (above_im, 1, 1), (below_im, 1, 3), (above_re, 0, 1),
        (opposite_re, 0, 2), (opposite_im, 1, 2),
    )
    opposite_re, opposite_im, part, pieces = tie((opposite_re, opposite_im, part, others(part, "y")))
    part = in_order(part, "y", pieces)
    other = swap(part)
    probe_gradient = jnp.concatenate([
        jnp.where(core == 0, part, other), jnp.where(core == 0, other, part)
    ], axis=1)
    whole = jnp.zeros((2, 2, 4, 2, SLICE, COLS), F32)

    def put(whole, block, plane, shift, owner):
        at = (plane, 0, lax.rem(z + shift, 4), owner, 0, 0)
        return lax.dynamic_update_slice(whole, block[None, :, None, None], at)

    for group in (found[:6], found[6:]):
        for block, plane, shift in group:
            whole = put(whole, block, plane, shift, core)
        for block, plane, shift in group:
            whole = put(whole, swap(block), plane, shift, 1 - core)
    return (whole.reshape(2, STRIP, COLS), probe_gradient)


def solution(mesh):
    tiles, scans = mesh.devices.shape
    side = math.isqrt(tiles)
    fine = Mesh(mesh.devices.reshape(side, tiles // side, scans // 2, 2), ("x", "y", "z", "core"))
    placed = (
        P(None, ("x", "y"), None),
        P(),
        P(("x", "y", "z", "core"), None, None),
        P(("x", "y", "z", "core"), None),
    )
    return jax.shard_map(
        on_device,
        mesh=fine,
        in_specs=placed,
        out_specs=(P(None, ("x", "y"), None), P()),
        check_vma=False,
    )
```

time: 1040 us -> 228 us (0.22)
  waiting for transfers between devices: 491 us -> 57.1 us
  matrix products: 383 us -> 8.35 us
  starting transfers between devices: 6.87 us -> 86.9 us
  local copies, waits for them, and re-layouts: 73.1 us -> 16.2 us
  Pallas kernels: 0 us -> 44.1 us
  other arithmetic: 41 us -> 13.8 us
  loops' own time: 25.5 us -> 0 us
  between operations: 14.3 us -> 1.46 us
    dot_general x48 -> x2, matrix products: 383 us -> 8.35 us  [the longest x1 4.35 us: on_device(): product('nkl,ml->nkm', product('mk,nkl->nml', order, amplitudes), order)]
    psum x2 -> x0, waiting for transfers between devices: 219 us -> none  [the longest x1 114 us: on_device(): probe_gradient = lax.psum(probe_sum, ('tile', 'scan'))]
    ppermute x2 -> x56, waiting for transfers between devices: 272 us -> 57.1 us  [the longest x10 32.3 us: z_up(): return lax.ppermute(block, 'z', ring('z', 1))]
    ppermute x2 -> x56, starting transfers between devices: 6.79 us -> 86.9 us  [the longest x19 30 us: swap(): return lax.ppermute(block, 'core', [(0, 1), (1, 0)])]
    pallas_call x0 -> x1, Pallas kernels: none -> 44.1 us  [run_patterns(): pl.pallas_call(patterns_kernel, out_shape=part + [jax.ShapeDtypeStruct((2...]
    dynamic_update_slice x3 -> x17, local copies, waits for them, and re-layouts: 42.6 us -> 5.59 us  [put(): return lax.dynamic_update_slice(whole, block[None, :, None, None], at)]
    another operation x1 -> x0, loops' own time: 25.5 us -> none  [on_device(): lax.scan(accumulate, start_totals, jnp.arange(pattern_count, dtype=jnp.in...]
    add x7 -> x12, other arithmetic: 24.3 us -> 9.3 us  [the longest x3 3.33 us: first_half(): both = mine + swap(theirs)]
  transfers between devices with their start and end apart: 4 -> 56, of which waited for: 4 -> 24; matrix products, arithmetic and copies ran while one was open for 1% -> 12% of each run, Pallas kernels for 0% -> 0%
where the time goes in v1:
time: 228 us
  starting transfers between devices  86.9 us (38%)
  waiting for transfers between devices  57.1 us (25%)
  Pallas kernels  44.1 us (19%)
  local copies, waits for them, and re-layouts  16.2 us (7%)
  other arithmetic  13.8 us (6%)
  matrix products  8.35 us (4%)
    pallas_call x1, Pallas kernels, run_patterns(): pl.pallas_call(patterns_kernel, out_shape=part + [jax.ShapeDtypeStruct((2...  44.1 us
    ppermute x10, waiting for transfers between devices, z_up(): return lax.ppermute(block, 'z', ring('z', 1))  32.3 us
    ppermute x19, starting transfers between devices, swap(): return lax.ppermute(block, 'core', [(0, 1), (1, 0)])  30 us
    ppermute x10, starting transfers between devices, z_down(): return lax.ppermute(block, 'z', ring('z', -1))  22.5 us
    ppermute x6, starting transfers between devices, share_of_sum(): lax.ppermute(lax.dynamic_index_in_dim(cut, lax.rem(here + step, 4), 1, ke...  14.6 us
    ppermute x9, starting transfers between devices, others(): return [lax.ppermute(block, axis, ring(axis, -step)) for step in (1, 2, 3)]  9.37 us
    ppermute x9, waiting for transfers between devices, others(): return [lax.ppermute(block, axis, ring(axis, -step)) for step in (1, 2, 3)]  8.08 us
    ppermute x19, waiting for transfers between devices, swap(): return lax.ppermute(block, 'core', [(0, 1), (1, 0)])  6.99 us
  transfers between devices with their start and end apart: 56, of which 24 were waited for; matrix products, arithmetic and copies ran while one was open for 12% of the time, Pallas kernels for 0%

profile of v1, /device:TPU:1, one launch (start us, length us, event | category | flops | bytes accessed | tf_op | source)
XLA Modules:
  0.0 227.9 jit_solution(8391413600799590054)
XLA Ops:
  3.4 4.0 %fusion.15 = f32[512,3,512]{2,0,1:T(8,128)S(1)} fusion(f32[512,512,1]{1,0,2:T(8,128)} %constant.146, f32[3,512,512]{2,1,0:T(8,128)S(1)} %copy-done), kind=kOutput, calls=%fused_computation.90 | convolution fusion | flops 2415919104 | bytes 7340032 | tf_op jit(solution)/shard_map/mk,nkl->nml/dot_general | solution.py:357
  7.4 4.3 %fusion.refs_11_ = f32[3,512,512]{2,1,0:T(8,128)} fusion(f32[512,512,1]{1,0,2:T(8,128)S(1)} %copy-done.3, f32[512,3,512]{2,0,1:T(8,128)S(1)} %fusion.15), kind=kOutput, calls=%fused_computation | convolution fusion | flops 2415919104 | bytes 7340032 | tf_op jit(solution)/shard_map/nkl,ml->nkm/dot_general | solution.py:357
  11.7 5.6 %collective-permute-done.refs_0_ = f32[2,64,1024]{2,1,0:T(8,128)S(1)} collective-permute-done((f32[2,64,1024]{2,1,0:T(8,128)S(1)}, f32[2,64,1024]{2,1,0:T(8,128)S(1)}, u32[]{:S(2)}, u32[]{:S(2)}) %collective-permute-start) | collective-permute-done | bytes 524320 | tf_op jit(solution)/shard_map/ppermute | solution.py:302
  19.2 2.1 collective-permute-start.2
  21.3 10.7 %collective-permute-done.1.refs_1_ = f32[2,64,1024]{2,1,0:T(8,128)S(1)} collective-permute-done((f32[2,64,1024]{2,1,0:T(8,128)S(1)}, f32[2,64,1024]{2,1,0:T(8,128)S(1)}, u32[]{:S(2)}, u32[]{:S(2)}) %collective-permute-start.1) | collective-permute-done | bytes 524320 | tf_op jit(solution)/shard_map/ppermute | solution.py:289
  32.2 2.7 %collective-permute-start.4 = (f32[64,1024]{1,0:T(8,128)S(1)}, f32[64,1024]{1,0:T(8,128)S(1)}, u32[]{:S(2)}, u32[]{:S(2)}) collective-permute-start(f32[64,1024]{1,0:T(8,128)S(1)} %slice_bitcast_fusion.11), channel_id=1, source_target_pairs={{0,6},{2,0},{4,2},{6,4},{1,7},{3,1},{5,3},{7,5},{8,14},{10,8},{12,... | collective-permute-start | bytes 786440 | tf_op jit(solution)/shard_map/ppermute | solution.py:293
  34.9 2.7 %collective-permute-start.5 = (f32[2,64,1024]{2,1,0:T(8,128)}, f32[2,64,1024]{2,1,0:T(8,128)S(1)}, u32[]{:S(2)}, u32[]{:S(2)}) collective-permute-start(f32[2,64,1024]{2,1,0:T(8,128)} %copy-done.12), channel_id=1, source_target_pairs={{0,1},{1,0},{2,3},{3,2},{4,5},{5,4},{6,7},{7,6},{8,9},{9,8},{10,11... | collective-permute-start | bytes 1572872 | tf_op jit(solution)/shard_map/ppermute | solution.py:297
  38.9 3.1 %collective-permute-start.8 = (f32[64,1024]{1,0:T(8,128)S(1)}, f32[64,1024]{1,0:T(8,128)}, u32[]{:S(2)}, u32[]{:S(2)}) collective-permute-start(f32[64,1024]{1,0:T(8,128)S(1)} %collective-permute-done.3.refs_3_), channel_id=1, source_target_pairs={{0,1},{1,0},{2,3},{3,2},{4,5},{5,4},{6,7},{7,6},{8,9},{9,8},{10,11... | collective-permute-start | bytes 786440 | tf_op jit(solution)/shard_map/ppermute | solution.py:297
  44.8 44.1 %shard_map.95 = (f32[2,2,64,1024]{3,2,1,0:T(8,128)}, f32[2,2,64,1024]{3,2,1,0:T(8,128)}, f32[2,2,64,1024]{3,2,1,0:T(8,128)}, f32[2,2,64,1024]{3,2,1,0:T(8,128)},...) custom-call(s32[8]{0:T(128)} %pad_add_fusion.where, ...), custom_call_target="tpu_custom_call" | custom-call | flops 9663676416 | bytes 40000000 | tf_op jit(solution)/shard_map/pallas_call | solution.py:264
  90.0 2.2 dynamic-slice_bitcast_fusion
  92.5 3.4 %collective-permute-done.14 = f32[2,2,64,1024]{3,2,1,0:T(8,128)S(1)} collective-permute-done((f32[2,2,64,1024]{3,2,1,0:T(8,128)}, f32[2,2,64,1024]{3,2,1,0:T(8,128)S(1)}, u32[]{:S(2)}, u32[]{:S(2)}) %collective-permute-start.14) | collective-permute-done | bytes 1048608 | tf_op jit(solution)/shard_map/ppermute | solution.py:297
  100.0 3.0 %collective-permute-start.16 = (f32[2,64,1024]{2,1,0:T(8,128)S(1)}, f32[2,64,1024]{2,1,0:T(8,128)S(1)}, u32[]{:S(2)}, u32[]{:S(2)}) collective-permute-start(f32[2,64,1024]{2,1,0:T(8,128)S(1)} %get-tuple-element.128), channel_id=1, source_target_pairs={{0,6},{2,0},{4,2},{6,4},{1,7},{3,1},{5,3},{7,5},{8,14},{10,8},{12,... | collective-permute-start | bytes 1572872 | tf_op jit(solution)/shard_map/ppermute | solution.py:293
  104.9 2.6 %collective-permute-start.13 = (f32[2,64,1024]{2,1,0:T(8,128)S(1)}, f32[2,64,1024]{2,1,0:T(8,128)S(1)}, u32[]{:S(2)}, u32[]{:S(2)}) collective-permute-start(f32[2,64,1024]{2,1,0:T(8,128)S(1)} %get-tuple-element.130), channel_id=1, source_target_pairs={{0,6},{2,0},{4,2},{6,4},{1,7},{3,1},{5,3},{7,5},{8,14},{10,8},{12,... | collective-permute-start | bytes 1572872 | tf_op jit(solution)/shard_map/ppermute | solution.py:293
  109.0 6.0 %collective-permute-done.15 = f32[2,64,1024]{2,1,0:T(8,128)S(1)} collective-permute-done((f32[2,64,1024]{2,1,0:T(8,128)S(1)}, f32[2,64,1024]{2,1,0:T(8,128)S(1)}, u32[]{:S(2)}, u32[]{:S(2)}) %collective-permute-start.15) | collective-permute-done | bytes 524320 | tf_op jit(solution)/shard_map/ppermute | solution.py:289
  116.4 4.7 %collective-permute-start.19 = (f32[2,64,512]{2,1,0:T(8,128)S(1)}, f32[2,64,512]{2,1,0:T(8,128)S(1)}, u32[]{:S(2)}, u32[]{:S(2)}) collective-permute-start(f32[2,64,512]{2,1,0:T(8,128)S(1)} %get-tuple-element.125), channel_id=1, source_target_pairs={{0,16},{8,24},{16,0},{24,8},{1,17},{9,25},{17,1},{25,9},{2,18},{10... | collective-permute-start | bytes 786440 | tf_op jit(solution)/shard_map/ppermute | solution.py:338
  121.2 2.8 %add.232 = f32[4,3,64,1024]{3,2,1,0:T(8,128)S(1)} add(f32[4,3,64,1024]{3,2,1,0:T(8,128)S(1)} %copy-done.4, f32[4,3,64,1024]{3,2,1,0:T(8,128)} %collective-permute-done.10) | non-fusion elementwise | flops 786432 | bytes 9437184 | tf_op jit(solution)/shard_map/add | solution.py:372
  127.8 2.4 %collective-permute-start.23 = (f32[2,64,1024]{2,1,0:T(8,128)S(1)}, f32[2,64,1024]{2,1,0:T(8,128)S(1)}, u32[]{:S(2)}, u32[]{:S(2)}) collective-permute-start(f32[2,64,1024]{2,1,0:T(8,128)S(1)} %get-tuple-element.132), channel_id=1, source_target_pairs={{0,6},{2,0},{4,2},{6,4},{1,7},{3,1},{5,3},{7,5},{8,14},{10,8},{12,... | collective-permute-start | bytes 1572872 | tf_op jit(solution)/shard_map/ppermute | solution.py:293
  135.4 2.7 %collective-permute-start.25 = (f32[2,16,512]{2,1,0:T(8,128)S(1)}, f32[2,16,512]{2,1,0:T(8,128)S(1)}, u32[]{:S(2)}, u32[]{:S(2)}) collective-permute-start(f32[2,16,512]{2,1,0:T(8,128)S(1)} %get-tuple-element.137), channel_id=1, source_target_pairs={{0,64},{32,96},{64,0},{96,32},{1,65},{33,97},{65,1},{97,33},{2,66}... | collective-permute-start | bytes 196616 | tf_op jit(solution)/shard_map/ppermute | solution.py:338
  138.2 7.4 %collective-permute-done.27 = f32[64,1024]{1,0:T(8,128)S(1)} collective-permute-done((f32[64,1024]{1,0:T(8,128)S(1)}, f32[64,1024]{1,0:T(8,128)S(1)}, u32[]{:S(2)}, u32[]{:S(2)}) %collective-permute-start.27) | collective-permute-done | bytes 262176 | tf_op jit(solution)/shard_map/ppermute | solution.py:289
  145.6 4.0 %collective-permute-start.26 = (f32[2,16,512]{2,1,0:T(8,128)S(1)}, f32[2,16,512]{2,1,0:T(8,128)S(1)}, u32[]{:S(2)}, u32[]{:S(2)}) collective-permute-start(f32[2,16,512]{2,1,0:T(8,128)S(1)} %get-tuple-element.136), channel_id=1, source_target_pairs={{0,96},{32,0},{64,32},{96,64},{1,97},{33,1},{65,33},{97,65},{2,98}... | collective-permute-start | bytes 196616 | tf_op jit(solution)/shard_map/ppermute | solution.py:338
  152.5 2.5 %collective-permute-start.37 = (f32[2,64,1024]{2,1,0:T(8,128)S(1)}, f32[2,64,1024]{2,1,0:T(8,128)S(1)}, u32[]{:S(2)}, u32[]{:S(2)}) collective-permute-start(f32[2,64,1024]{2,1,0:T(8,128)S(1)} %pad_maximum_fusion.3), channel_id=1, source_target_pairs={{0,8},{8,16},{16,24},{24,32},{32,40},{40,48},{48,56},{56,64},{64,7... | collective-permute-start | bytes 1572872 | tf_op jit(solution)/shard_map/ppermute | solution.py:302
  156.6 3.1 %collective-permute-start.34 = (f32[2,16,512]{2,1,0:T(8,128)S(1)}, f32[2,16,512]{2,1,0:T(8,128)S(1)}, u32[]{:S(2)}, u32[]{:S(2)}) collective-permute-start(f32[2,16,512]{2,1,0:T(8,128)S(1)} %get-tuple-element.115), channel_id=1, source_target_pairs={{0,96},{32,0},{64,32},{96,64},{1,97},{33,1},{65,33},{97,65},{2,98}... | collective-permute-start | bytes 196616 | tf_op jit(solution)/shard_map/ppermute | solution.py:323
  164.7 5.3 %collective-permute-done.32 = f32[2,64,1024]{2,1,0:T(8,128)S(1)} collective-permute-done((f32[2,64,1024]{2,1,0:T(8,128)S(1)}, f32[2,64,1024]{2,1,0:T(8,128)S(1)}, u32[]{:S(2)}, u32[]{:S(2)}) %collective-permute-start.32) | collective-permute-done | bytes 524320 | tf_op jit(solution)/shard_map/ppermute | solution.py:289
  175.9 2.7 %collective-permute-start.41 = (f32[2,64,1024]{2,1,0:T(8,128)}, f32[2,64,1024]{2,1,0:T(8,128)S(1)}, u32[]{:S(2)}, u32[]{:S(2)}) collective-permute-start(f32[2,64,1024]{2,1,0:T(8,128)} %get-tuple-element.107), channel_id=1, source_target_pairs={{0,6},{2,0},{4,2},{6,4},{1,7},{3,1},{5,3},{7,5},{8,14},{10,8},{12,... | collective-permute-start | bytes 1572872 | tf_op jit(solution)/shard_map/ppermute | solution.py:293
  178.6 7.6 %collective-permute-start.42 = (f32[2,64,1024]{2,1,0:T(8,128)}, f32[2,64,1024]{2,1,0:T(8,128)S(1)}, u32[]{:S(2)}, u32[]{:S(2)}) collective-permute-start(f32[2,64,1024]{2,1,0:T(8,128)} %get-tuple-element.107), channel_id=1, source_target_pairs={{0,1},{1,0},{2,3},{3,2},{4,5},{5,4},{6,7},{7,6},{8,9},{9,8},{10,11... | collective-permute-start | bytes 1572872 | tf_op jit(solution)/shard_map/ppermute | solution.py:297
  189.4 5.3 %collective-permute-start.43 = (f32[2,64,1024]{2,1,0:T(8,128)}, f32[2,64,1024]{2,1,0:T(8,128)S(1)}, u32[]{:S(2)}, u32[]{:S(2)}) collective-permute-start(f32[2,64,1024]{2,1,0:T(8,128)} %get-tuple-element.108), channel_id=1, source_target_pairs={{0,1},{1,0},{2,3},{3,2},{4,5},{5,4},{6,7},{7,6},{8,9},{9,8},{10,11... | collective-permute-start | bytes 1572872 | tf_op jit(solution)/shard_map/ppermute | solution.py:297
  195.8 3.4 %collective-permute-start.52 = (f32[2,64,512]{2,1,0:T(8,128)S(1)}, f32[2,64,512]{2,1,0:T(8,128)S(1)}, u32[]{:S(2)}, u32[]{:S(2)}) collective-permute-start(f32[2,64,512]{2,1,0:T(8,128)S(1)} %bitcast.197), channel_id=1, source_target_pairs={{0,24},{8,0},{16,8},{24,16},{1,25},{9,1},{17,9},{25,17},{2,26},{10... | collective-permute-start | bytes 786440 | tf_op jit(solution)/shard_map/ppermute | solution.py:323
  199.4 2.7 %collective-permute-start.49 = (f32[2,64,1024]{2,1,0:T(8,128)S(1)}, f32[2,64,1024]{2,1,0:T(8,128)S(1)}, u32[]{:S(2)}, u32[]{:S(2)}) collective-permute-start(f32[2,64,1024]{2,1,0:T(8,128)S(1)} %collective-permute-done.39), channel_id=1, source_target_pairs={{0,6},{2,0},{4,2},{6,4},{1,7},{3,1},{5,3},{7,5},{8,14},{10,8},{12,... | collective-permute-start | bytes 1572872 | tf_op jit(solution)/shard_map/ppermute | solution.py:293
  204.8 3.0 %collective-permute-done.52 = f32[2,64,512]{2,1,0:T(8,128)S(1)} collective-permute-done((f32[2,64,512]{2,1,0:T(8,128)S(1)}, f32[2,64,512]{2,1,0:T(8,128)S(1)}, u32[]{:S(2)}, u32[]{:S(2)}) %collective-permute-start.52) | collective-permute-done | bytes 262176 | tf_op jit(solution)/shard_map/ppermute | solution.py:323
  207.8 2.3 %collective-permute-start.44 = (f32[2,64,1024]{2,1,0:T(8,128)}, f32[2,64,1024]{2,1,0:T(8,128)S(1)}, u32[]{:S(2)}, u32[]{:S(2)}) collective-permute-start(f32[2,64,1024]{2,1,0:T(8,128)} %collective-permute-done.38), channel_id=1, source_target_pairs={{0,1},{1,0},{2,3},{3,2},{4,5},{5,4},{6,7},{7,6},{8,9},{9,8},{10,11... | collective-permute-start | bytes 1572872 | tf_op jit(solution)/shard_map/ppermute | solution.py:297
  210.2 4.3 %collective-permute-start.45 = (f32[2,64,1024]{2,1,0:T(8,128)S(1)}, f32[2,64,1024]{2,1,0:T(8,128)S(1)}, u32[]{:S(2)}, u32[]{:S(2)}) collective-permute-start(f32[2,64,1024]{2,1,0:T(8,128)S(1)} %collective-permute-done.39), channel_id=1, source_target_pairs={{0,1},{1,0},{2,3},{3,2},{4,5},{5,4},{6,7},{7,6},{8,9},{9,8},{10,11... | collective-permute-start | bytes 1572872 | tf_op jit(solution)/shard_map/ppermute | solution.py:297
  225.1 2.7 %copy-done.2 = f32[2,2,4,2,64,1024]{5,4,3,2,1,0:T(8,128)} copy-done((f32[2,2,4,2,64,1024]{5,4,3,2,1,0:T(8,128)}, f32[2,2,4,2,64,1024]{5,4,3,2,1,0:T(8,128)S(1)}, u32[]{:S(2)}) %copy-start.2) | copy-done | bytes 8388632
  (190 shorter events, 61.0 us)
Async XLA Ops:
  1.9 15.4 %collective-permute-start = (f32[2,64,1024]{2,1,0:T(8,128)S(1)}, f32[2,64,1024]{2,1,0:T(8,128)S(1)}, u32[]{:S(2)}, u32[]{:S(2)}) collective-permute-start(f32[2,64,1024]{2,1,0:T(8,128)S(1)} %constant_dynamic-slice_fusion.2), channel_id=1, source_target_pairs={{8,0},{16,8},{24,16},{32,24},{40,32},{48,40},{56,48},{64,56},{72,6... | collective-permute-start | bytes 1572872 | tf_op jit(solution)/shard_map/ppermute | solution.py:302
  17.3 14.7 %collective-permute-start.1 = (f32[2,64,1024]{2,1,0:T(8,128)S(1)}, f32[2,64,1024]{2,1,0:T(8,128)S(1)}, u32[]{:S(2)}, u32[]{:S(2)}) collective-permute-start(f32[2,64,1024]{2,1,0:T(8,128)S(1)} %collective-permute-done.refs_0_), channel_id=1, source_target_pairs={{0,2},{2,4},{4,6},{6,0},{1,3},{3,5},{5,7},{7,1},{8,10},{10,12},{12... | collective-permute-start | bytes 1572872 | tf_op jit(solution)/shard_map/ppermute | solution.py:289
  19.2 12.9 %collective-permute-start.2 = (f32[2,64,1024]{2,1,0:T(8,128)S(1)}, f32[2,64,1024]{2,1,0:T(8,128)S(1)}, u32[]{:S(2)}, u32[]{:S(2)}) collective-permute-start(f32[2,64,1024]{2,1,0:T(8,128)S(1)} %collective-permute-done.refs_0_), channel_id=1, source_target_pairs={{0,6},{2,0},{4,2},{6,4},{1,7},{3,1},{5,3},{7,5},{8,14},{10,8},{12,... | collective-permute-start | bytes 1572872 | tf_op jit(solution)/shard_map/ppermute | solution.py:293
  32.2 9.9 %collective-permute-start.4 = (f32[64,1024]{1,0:T(8,128)S(1)}, f32[64,1024]{1,0:T(8,128)S(1)}, u32[]{:S(2)}, u32[]{:S(2)}) collective-permute-start(f32[64,1024]{1,0:T(8,128)S(1)} %slice_bitcast_fusion.11), channel_id=1, source_target_pairs={{0,6},{2,0},{4,2},{6,4},{1,7},{3,1},{5,3},{7,5},{8,14},{10,8},{12,... | collective-permute-start | bytes 786440 | tf_op jit(solution)/shard_map/ppermute | solution.py:293
  88.9 32.3 %collective-permute-start.10 = (f32[4,3,64,1024]{3,2,1,0:T(8,128)}, f32[4,3,64,1024]{3,2,1,0:T(8,128)}, u32[]{:S(2)}, u32[]{:S(2)}) collective-permute-start(f32[4,3,64,1024]{3,2,1,0:T(8,128)} %get-tuple-element.73), channel_id=1, source_target_pairs={{0,1},{1,0},{2,3},{3,2},{4,5},{5,4},{6,7},{7,6},{8,9},{9,8},{10,11... | collective-permute-start | bytes 9437192 | tf_op jit(solution)/shard_map/ppermute | solution.py:297
  89.5 10.6 %collective-permute-start.11 = (f32[2,2,64,1024]{3,2,1,0:T(8,128)}, f32[2,2,64,1024]{3,2,1,0:T(8,128)S(1)}, u32[]{:S(2)}, u32[]{:S(2)}) collective-permute-start(f32[2,2,64,1024]{3,2,1,0:T(8,128)} %get-tuple-element.75), channel_id=1, source_target_pairs={{0,1},{1,0},{2,3},{3,2},{4,5},{5,4},{6,7},{7,6},{8,9},{9,8},{10,11... | collective-permute-start | bytes 3145736 | tf_op jit(solution)/shard_map/ppermute | solution.py:297
  89.7 13.6 %collective-permute-start.21 = (f32[2,2,64,1024]{3,2,1,0:T(8,128)}, f32[2,2,64,1024]{3,2,1,0:T(8,128)}, u32[]{:S(2)}, u32[]{:S(2)}) collective-permute-start(f32[2,2,64,1024]{3,2,1,0:T(8,128)} %get-tuple-element.82), channel_id=1, source_target_pairs={{0,1},{1,0},{2,3},{3,2},{4,5},{5,4},{6,7},{7,6},{8,9},{9,8},{10,11... | collective-permute-start | bytes 3145736 | tf_op jit(solution)/shard_map/ppermute | solution.py:297
  92.2 12.7 %collective-permute-start.17 = (f32[2,256,512]{2,1,0:T(8,128)}, f32[2,256,512]{2,1,0:T(8,128)}, u32[]{:S(2)}, u32[]{:S(2)}) collective-permute-start(f32[2,256,512]{2,1,0:T(8,128)} %dynamic-slice_bitcast_fusion), channel_id=1, source_target_pairs={{0,1},{1,0},{2,3},{3,2},{4,5},{5,4},{6,7},{7,6},{8,9},{9,8},{10,11... | collective-permute-start | bytes 3145736 | tf_op jit(solution)/shard_map/ppermute | solution.py:297
  98.6 16.3 %collective-permute-start.15 = (f32[2,64,1024]{2,1,0:T(8,128)S(1)}, f32[2,64,1024]{2,1,0:T(8,128)S(1)}, u32[]{:S(2)}, u32[]{:S(2)}) collective-permute-start(f32[2,64,1024]{2,1,0:T(8,128)S(1)} %get-tuple-element.129), channel_id=1, source_target_pairs={{0,2},{2,4},{4,6},{6,0},{1,3},{3,5},{5,7},{7,1},{8,10},{10,12},{12... | collective-permute-start | bytes 1572872 | tf_op jit(solution)/shard_map/ppermute | solution.py:289
  100.0 14.9 %collective-permute-start.16 = (f32[2,64,1024]{2,1,0:T(8,128)S(1)}, f32[2,64,1024]{2,1,0:T(8,128)S(1)}, u32[]{:S(2)}, u32[]{:S(2)}) collective-permute-start(f32[2,64,1024]{2,1,0:T(8,128)S(1)} %get-tuple-element.128), channel_id=1, source_target_pairs={{0,6},{2,0},{4,2},{6,4},{1,7},{3,1},{5,3},{7,5},{8,14},{10,8},{12,... | collective-permute-start | bytes 1572872 | tf_op jit(solution)/shard_map/ppermute | solution.py:293
  103.3 22.8 %collective-permute-start.12 = (f32[2,64,1024]{2,1,0:T(8,128)S(1)}, f32[2,64,1024]{2,1,0:T(8,128)S(1)}, u32[]{:S(2)}, u32[]{:S(2)}) collective-permute-start(f32[2,64,1024]{2,1,0:T(8,128)S(1)} %get-tuple-element.131), channel_id=1, source_target_pairs={{0,2},{2,4},{4,6},{6,0},{1,3},{3,5},{5,7},{7,1},{8,10},{10,12},{12... | collective-permute-start | bytes 1572872 | tf_op jit(solution)/shard_map/ppermute | solution.py:289
  104.9 22.5 %collective-permute-start.13 = (f32[2,64,1024]{2,1,0:T(8,128)S(1)}, f32[2,64,1024]{2,1,0:T(8,128)S(1)}, u32[]{:S(2)}, u32[]{:S(2)}) collective-permute-start(f32[2,64,1024]{2,1,0:T(8,128)S(1)} %get-tuple-element.130), channel_id=1, source_target_pairs={{0,6},{2,0},{4,2},{6,4},{1,7},{3,1},{5,3},{7,5},{8,14},{10,8},{12,... | collective-permute-start | bytes 1572872 | tf_op jit(solution)/shard_map/ppermute | solution.py:293
  115.0 12.8 %collective-permute-start.18 = (f32[2,64,512]{2,1,0:T(8,128)S(1)}, f32[2,64,512]{2,1,0:T(8,128)S(1)}, u32[]{:S(2)}, u32[]{:S(2)}) collective-permute-start(f32[2,64,512]{2,1,0:T(8,128)S(1)} %get-tuple-element.126), channel_id=1, source_target_pairs={{0,8},{8,16},{16,24},{24,0},{1,9},{9,17},{17,25},{25,1},{2,10},{10... | collective-permute-start | bytes 786440 | tf_op jit(solution)/shard_map/ppermute | solution.py:338
  116.4 15.3 %collective-permute-start.19 = (f32[2,64,512]{2,1,0:T(8,128)S(1)}, f32[2,64,512]{2,1,0:T(8,128)S(1)}, u32[]{:S(2)}, u32[]{:S(2)}) collective-permute-start(f32[2,64,512]{2,1,0:T(8,128)S(1)} %get-tuple-element.125), channel_id=1, source_target_pairs={{0,16},{8,24},{16,0},{24,8},{1,17},{9,25},{17,1},{25,9},{2,18},{10... | collective-permute-start | bytes 786440 | tf_op jit(solution)/shard_map/ppermute | solution.py:338
  121.2 10.8 %collective-permute-start.20 = (f32[2,64,512]{2,1,0:T(8,128)S(1)}, f32[2,64,512]{2,1,0:T(8,128)S(1)}, u32[]{:S(2)}, u32[]{:S(2)}) collective-permute-start(f32[2,64,512]{2,1,0:T(8,128)S(1)} %get-tuple-element.124), channel_id=1, source_target_pairs={{0,24},{8,0},{16,8},{24,16},{1,25},{9,1},{17,9},{25,17},{2,26},{10... | collective-permute-start | bytes 786440 | tf_op jit(solution)/shard_map/ppermute | solution.py:338
  127.4 22.2 %collective-permute-start.22 = (f32[2,64,1024]{2,1,0:T(8,128)S(1)}, f32[2,64,1024]{2,1,0:T(8,128)S(1)}, u32[]{:S(2)}, u32[]{:S(2)}) collective-permute-start(f32[2,64,1024]{2,1,0:T(8,128)S(1)} %get-tuple-element.133), channel_id=1, source_target_pairs={{0,2},{2,4},{4,6},{6,0},{1,3},{3,5},{5,7},{7,1},{8,10},{10,12},{12... | collective-permute-start | bytes 1572872 | tf_op jit(solution)/shard_map/ppermute | solution.py:289
  127.8 21.8 %collective-permute-start.23 = (f32[2,64,1024]{2,1,0:T(8,128)S(1)}, f32[2,64,1024]{2,1,0:T(8,128)S(1)}, u32[]{:S(2)}, u32[]{:S(2)}) collective-permute-start(f32[2,64,1024]{2,1,0:T(8,128)S(1)} %get-tuple-element.132), channel_id=1, source_target_pairs={{0,6},{2,0},{4,2},{6,4},{1,7},{3,1},{5,3},{7,5},{8,14},{10,8},{12,... | collective-permute-start | bytes 1572872 | tf_op jit(solution)/shard_map/ppermute | solution.py:293
  133.2 12.4 %collective-permute-start.27 = (f32[64,1024]{1,0:T(8,128)S(1)}, f32[64,1024]{1,0:T(8,128)S(1)}, u32[]{:S(2)}, u32[]{:S(2)}) collective-permute-start(f32[64,1024]{1,0:T(8,128)S(1)} %get-tuple-element.117), channel_id=1, source_target_pairs={{0,2},{2,4},{4,6},{6,0},{1,3},{3,5},{5,7},{7,1},{8,10},{10,12},{12... | collective-permute-start | bytes 786440 | tf_op jit(solution)/shard_map/ppermute | solution.py:289
  133.6 16.0 %collective-permute-start.24 = (f32[2,16,512]{2,1,0:T(8,128)S(1)}, f32[2,16,512]{2,1,0:T(8,128)S(1)}, u32[]{:S(2)}, u32[]{:S(2)}) collective-permute-start(f32[2,16,512]{2,1,0:T(8,128)S(1)} %get-tuple-element.138), channel_id=1, source_target_pairs={{0,32},{32,64},{64,96},{96,0},{1,33},{33,65},{65,97},{97,1},{2,34}... | collective-permute-start | bytes 196616 | tf_op jit(solution)/shard_map/ppermute | solution.py:338
  135.4 14.2 %collective-permute-start.25 = (f32[2,16,512]{2,1,0:T(8,128)S(1)}, f32[2,16,512]{2,1,0:T(8,128)S(1)}, u32[]{:S(2)}, u32[]{:S(2)}) collective-permute-start(f32[2,16,512]{2,1,0:T(8,128)S(1)} %get-tuple-element.137), channel_id=1, source_target_pairs={{0,64},{32,96},{64,0},{96,32},{1,65},{33,97},{65,1},{97,33},{2,66}... | collective-permute-start | bytes 196616 | tf_op jit(solution)/shard_map/ppermute | solution.py:338
  152.5 18.9 %collective-permute-start.37 = (f32[2,64,1024]{2,1,0:T(8,128)S(1)}, f32[2,64,1024]{2,1,0:T(8,128)S(1)}, u32[]{:S(2)}, u32[]{:S(2)}) collective-permute-start(f32[2,64,1024]{2,1,0:T(8,128)S(1)} %pad_maximum_fusion.3), channel_id=1, source_target_pairs={{0,8},{8,16},{16,24},{24,32},{32,40},{40,48},{48,56},{56,64},{64,7... | collective-permute-start | bytes 1572872 | tf_op jit(solution)/shard_map/ppermute | solution.py:302
  173.3 16.2 %collective-permute-start.38 = (f32[2,64,1024]{2,1,0:T(8,128)}, f32[2,64,1024]{2,1,0:T(8,128)}, u32[]{:S(2)}, u32[]{:S(2)}) collective-permute-start(f32[2,64,1024]{2,1,0:T(8,128)} %get-tuple-element.107), channel_id=1, source_target_pairs={{0,2},{2,4},{4,6},{6,0},{1,3},{3,5},{5,7},{7,1},{8,10},{10,12},{12... | collective-permute-start | bytes 1572872 | tf_op jit(solution)/shard_map/ppermute | solution.py:289
  174.3 21.6 %collective-permute-start.39 = (f32[2,64,1024]{2,1,0:T(8,128)}, f32[2,64,1024]{2,1,0:T(8,128)S(1)}, u32[]{:S(2)}, u32[]{:S(2)}) collective-permute-start(f32[2,64,1024]{2,1,0:T(8,128)} %get-tuple-element.108), channel_id=1, source_target_pairs={{0,6},{2,0},{4,2},{6,4},{1,7},{3,1},{5,3},{7,5},{8,14},{10,8},{12,... | collective-permute-start | bytes 1572872 | tf_op jit(solution)/shard_map/ppermute | solution.py:293
  175.9 23.3 %collective-permute-start.40 = (f32[2,64,1024]{2,1,0:T(8,128)}, f32[2,64,1024]{2,1,0:T(8,128)S(1)}, u32[]{:S(2)}, u32[]{:S(2)}) collective-permute-start(f32[2,64,1024]{2,1,0:T(8,128)} %get-tuple-element.108), channel_id=1, source_target_pairs={{0,2},{2,4},{4,6},{6,0},{1,3},{3,5},{5,7},{7,1},{8,10},{10,12},{12... | collective-permute-start | bytes 1572872 | tf_op jit(solution)/shard_map/ppermute | solution.py:289
  175.9 23.5 %collective-permute-start.41 = (f32[2,64,1024]{2,1,0:T(8,128)}, f32[2,64,1024]{2,1,0:T(8,128)S(1)}, u32[]{:S(2)}, u32[]{:S(2)}) collective-permute-start(f32[2,64,1024]{2,1,0:T(8,128)} %get-tuple-element.107), channel_id=1, source_target_pairs={{0,6},{2,0},{4,2},{6,4},{1,7},{3,1},{5,3},{7,5},{8,14},{10,8},{12,... | collective-permute-start | bytes 1572872 | tf_op jit(solution)/shard_map/ppermute | solution.py:293
  178.6 23.6 %collective-permute-start.42 = (f32[2,64,1024]{2,1,0:T(8,128)}, f32[2,64,1024]{2,1,0:T(8,128)S(1)}, u32[]{:S(2)}, u32[]{:S(2)}) collective-permute-start(f32[2,64,1024]{2,1,0:T(8,128)} %get-tuple-element.107), channel_id=1, source_target_pairs={{0,1},{1,0},{2,3},{3,2},{4,5},{5,4},{6,7},{7,6},{8,9},{9,8},{10,11... | collective-permute-start | bytes 1572872 | tf_op jit(solution)/shard_map/ppermute | solution.py:297
  189.4 12.9 %collective-permute-start.43 = (f32[2,64,1024]{2,1,0:T(8,128)}, f32[2,64,1024]{2,1,0:T(8,128)S(1)}, u32[]{:S(2)}, u32[]{:S(2)}) collective-permute-start(f32[2,64,1024]{2,1,0:T(8,128)} %get-tuple-element.108), channel_id=1, source_target_pairs={{0,1},{1,0},{2,3},{3,2},{4,5},{5,4},{6,7},{7,6},{8,9},{9,8},{10,11... | collective-permute-start | bytes 1572872 | tf_op jit(solution)/shard_map/ppermute | solution.py:297
  195.8 11.9 %collective-permute-start.52 = (f32[2,64,512]{2,1,0:T(8,128)S(1)}, f32[2,64,512]{2,1,0:T(8,128)S(1)}, u32[]{:S(2)}, u32[]{:S(2)}) collective-permute-start(f32[2,64,512]{2,1,0:T(8,128)S(1)} %bitcast.197), channel_id=1, source_target_pairs={{0,24},{8,0},{16,8},{24,16},{1,25},{9,1},{17,9},{25,17},{2,26},{10... | collective-permute-start | bytes 786440 | tf_op jit(solution)/shard_map/ppermute | solution.py:323
  199.3 18.7 %collective-permute-start.48 = (f32[2,64,1024]{2,1,0:T(8,128)}, f32[2,64,1024]{2,1,0:T(8,128)S(1)}, u32[]{:S(2)}, u32[]{:S(2)}) collective-permute-start(f32[2,64,1024]{2,1,0:T(8,128)} %collective-permute-done.38), channel_id=1, source_target_pairs={{0,2},{2,4},{4,6},{6,0},{1,3},{3,5},{5,7},{7,1},{8,10},{10,12},{12... | collective-permute-start | bytes 1572872 | tf_op jit(solution)/shard_map/ppermute | solution.py:289
  199.4 18.5 %collective-permute-start.49 = (f32[2,64,1024]{2,1,0:T(8,128)S(1)}, f32[2,64,1024]{2,1,0:T(8,128)S(1)}, u32[]{:S(2)}, u32[]{:S(2)}) collective-permute-start(f32[2,64,1024]{2,1,0:T(8,128)S(1)} %collective-permute-done.39), channel_id=1, source_target_pairs={{0,6},{2,0},{4,2},{6,4},{1,7},{3,1},{5,3},{7,5},{8,14},{10,8},{12,... | collective-permute-start | bytes 1572872 | tf_op jit(solution)/shard_map/ppermute | solution.py:293
  202.3 14.3 %collective-permute-start.54 = (f32[2,64,512]{2,1,0:T(8,128)S(1)}, f32[2,64,512]{2,1,0:T(8,128)S(1)}, u32[]{:S(2)}, u32[]{:S(2)}) collective-permute-start(f32[2,64,512]{2,1,0:T(8,128)S(1)} %bitcast.199), channel_id=1, source_target_pairs={{0,8},{8,16},{16,24},{24,0},{1,9},{9,17},{17,25},{25,1},{2,10},{10... | collective-permute-start | bytes 786440 | tf_op jit(solution)/shard_map/ppermute | solution.py:323
  207.8 11.3 %collective-permute-start.44 = (f32[2,64,1024]{2,1,0:T(8,128)}, f32[2,64,1024]{2,1,0:T(8,128)S(1)}, u32[]{:S(2)}, u32[]{:S(2)}) collective-permute-start(f32[2,64,1024]{2,1,0:T(8,128)} %collective-permute-done.38), channel_id=1, source_target_pairs={{0,1},{1,0},{2,3},{3,2},{4,5},{5,4},{6,7},{7,6},{8,9},{9,8},{10,11... | collective-permute-start | bytes 1572872 | tf_op jit(solution)/shard_map/ppermute | solution.py:297
  (43 other events, 298.6 us)
